TPU v7x, 32 devices: a whole 2x2x4 slice. The times are simulated.
32 devices in a mesh: groups: 2 (over y), ranks: 8 (over z, x), tp: 2 (over core).
Axes of the slice: x: 2, y: 2, z: 4, core: 2. Of those that a mesh axis runs over, the one named last changes fastest.
Arguments:
- queries: bfloat16 [128, 6144], P(('groups', 'ranks'), 'tp'), parts along dimension 0, may hold values from -8 to 8
- cache_keys: bfloat16 [1024, 16, 1024], P(('groups', 'ranks'), None, 'tp'), parts along dimension 0, may hold values from -1000 to 1000
- cache_values: bfloat16 [1024, 16, 1024], P(('groups', 'ranks'), None, 'tp'), parts along dimension 0, may hold values from -6 to 6
- fresh_keys: bfloat16 [128, 1024], P(('groups', 'ranks'), 'tp'), parts along dimension 0, may hold values from -7 to 7
- fresh_values: bfloat16 [128, 1024], P(('groups', 'ranks'), 'tp'), parts along dimension 0, may hold values from -6 to 6
- block_table: int32 [128, 8], P(('groups', 'ranks')), parts along dimension 0, may hold values from 0 to 63, as said below
- lengths: int32 [128], P(('groups', 'ranks')), parts along dimension 0, may hold values from 16 to 127, as said below
- stream: bfloat16 [128, 6144], P(('groups', 'ranks')), parts along dimension 0, may hold values from -2 to 2
- norm_gain: bfloat16 [6144], replicated, may hold values from 0.099609375 to 1.8984375
- router: bfloat16 [6144, 4], replicated, may hold values from -0.078125 to 0.078125
- routes: int32 [128, 2], P(('groups', 'ranks')), parts along dimension 0, may hold values from 0 to 3, all different within a row; in each aligned block of 8 rows (0 to 7, 8 to 15, ...) at most 6 rows name the same one
- expert_gate: bfloat16 [6144, 32768], P(None, ('ranks', 'tp')), may hold values from -0.078125 to 0.078125
- expert_up: bfloat16 [6144, 32768], P(None, ('ranks', 'tp')), may hold values from -0.078125 to 0.078125
- expert_down: bfloat16 [32768, 6144], P(('ranks', 'tp')), may hold values from -0.0625 to 0.0625
Outputs:
- layer_out: bfloat16 [128, 6144], P(('groups', 'ranks'), 'tp'), parts along dimension 0
- moved_keys: bfloat16 [16, 128, 1024], P(('groups', 'ranks'), None, 'tp'), parts along dimension 0
- moved_values: bfloat16 [16, 128, 1024], P(('groups', 'ranks'), None, 'tp'), parts along dimension 0
There are 2 independent parts, one for each index of `groups`. A program takes and returns all parts, laid end to end along the dimension named above; an argument that names none is the same for every part. Nothing has to cross between parts.
Inputs may be any that keep to these rules, and one draw needn't show every extreme that they name: `block_table`: the rows of each rank form a permutation of 0 to 63. `lengths`: some request has 127.
All inputs are finite; a program needn't handle non-finite values.
Results may differ from a plain program's by a relative error of at most 0.018.
Values may be sent and summed in bfloat16 or wider, within the bound.
A program may use at most 192 MiB of HBM per device.

v0:
```python
import jax
import jax.numpy as jnp
from jax import lax
from jax.sharding import PartitionSpec as P

HD = 128
CAP = 6


EPSILON = 1e-05


def shifted(value, axis, steps):
    count = lax.axis_size(axis)
    pairs = [(source, (source + steps) % count) for source in range(count)]
    return lax.ppermute(value, axis, pairs)


def logical_cache(pool_keys, pool_values, table, lengths, fresh_keys, fresh_values):
    requests, blocks = table.shape
    width = pool_keys.shape[2]
    context = blocks * pool_keys.shape[1]
    flat = table.reshape(-1)
    keys = pool_keys[flat].reshape(requests, context, width)
    values = pool_values[flat].reshape(requests, context, width)
    position = lax.broadcasted_iota(jnp.int32, (requests, context, 1), 1)
    limit = lengths.reshape(requests, 1, 1)
    keys = jnp.where(
        position < limit,
        keys,
        jnp.where(position == limit, fresh_keys[:, None, :], jnp.zeros_like(keys)),
    )
    values = jnp.where(
        position < limit,
        values,
        jnp.where(position == limit, fresh_values[:, None, :], jnp.zeros_like(values)),
    )
    return (keys, values)


def attend(query, keys, values, limit):
    requests, context, width = keys.shape
    groups = width // HD
    heads = query.shape[1] // HD
    share = heads // groups
    q_heads = query.reshape(requests, groups, share, HD)
    k_heads = keys.reshape(requests, context, groups, HD)
    v_heads = values.reshape(requests, context, groups, HD)
    scores = jnp.einsum(
        "rgqd,rpgd->rgqp", q_heads, k_heads, preferred_element_type=jnp.float32
    ) * HD ** (-0.5)
    position = lax.broadcasted_iota(jnp.int32, scores.shape, 3)
    scores = jnp.where(position <= limit.reshape(requests, 1, 1, 1), scores, -1e30)
    top = jnp.max(scores, axis=3, keepdims=True)
    powers = jnp.exp(scores - top)
    probs = (powers / jnp.sum(powers, axis=3, keepdims=True)).astype(jnp.bfloat16)
    mixed = jnp.einsum("rgqp,rpgd->rgqd", probs, v_heads, preferred_element_type=jnp.float32)
    return mixed.astype(jnp.bfloat16).reshape(requests, heads * HD)


def shards(
    queries,
    cache_keys,
    cache_values,
    fresh_keys,
    fresh_values,
    block_table,
    lengths,
    stream,
    norm_gain,
    router,
    routes,
    expert_gate,
    expert_up,
    expert_down,
):
    ranks = lax.axis_size("ranks")
    half_way = ranks // 2
    requests = queries.shape[0]
    keys, values = logical_cache(
        cache_keys, cache_values, block_table, lengths, fresh_keys, fresh_values
    )
    context = keys.shape[1]
    position_row = lax.broadcasted_iota(jnp.int32, (context,), 0)
    valid = (position_row <= lengths[0]).astype(jnp.bfloat16)
    moved_k, moved_v, moved_query, moved_stream, moved_valid = shifted(
        (keys[0], values[0], queries[0], stream[0], valid), "ranks", half_way
    )
    arrived = (jnp.sum(moved_valid.astype(jnp.float32)) - 1.0).astype(jnp.int32)
    keys_now = keys.at[0].set(moved_k)
    values_now = values.at[0].set(moved_v)
    query_now = queries.at[0].set(moved_query)
    stream_now = stream.at[0].set(moved_stream)
    limit_now = lengths.at[0].set(arrived)
    attn = attend(query_now, keys_now, values_now, limit_now)
    half = attn.shape[1]
    column = lax.axis_index("tp") * half
    own_stream = lax.dynamic_slice_in_dim(stream_now, column, half, 1)
    middle_part = (own_stream.astype(jnp.float32) + attn.astype(jnp.float32)).astype(jnp.bfloat16)
    middle = lax.all_gather(middle_part, "tp", axis=1, tiled=True)
    width = middle.shape[1]
    wide = middle.astype(jnp.float32)
    normed = (
        wide
        * lax.rsqrt(jnp.mean(wide * wide, axis=1, keepdims=True) + EPSILON)
        * norm_gain.astype(jnp.float32)
    ).astype(jnp.bfloat16)
    logits = jnp.dot(normed, router, preferred_element_type=jnp.float32)
    experts = router.shape[1]
    first = jnp.take_along_axis(logits, routes[:, 0:1], axis=1)[:, 0]
    second = jnp.take_along_axis(logits, routes[:, 1:2], axis=1)[:, 0]
    share_first = jax.nn.sigmoid(first - second)
    expert_ids = lax.broadcasted_iota(jnp.int32, (requests, experts), 1)
    chosen_first = routes[:, 0:1] == expert_ids
    chosen_second = routes[:, 1:2] == expert_ids
    member = (chosen_first | chosen_second).astype(jnp.int32)
    gating = jnp.where(chosen_first, share_first[:, None], 0.0) + jnp.where(
        chosen_second, (1.0 - share_first)[:, None], 0.0
    )
    place = jnp.cumsum(member, axis=0) - 1
    slot_ids = lax.broadcasted_iota(jnp.int32, (1, 1, CAP), 2)
    hit = (member[:, :, None] == 1) & (place[:, :, None] == slot_ids)
    select = hit.astype(jnp.bfloat16).reshape(requests, experts * CAP).T
    packed = (
        jnp.dot(select, normed, preferred_element_type=jnp.float32)
        .astype(jnp.bfloat16)
        .reshape(experts, CAP, width)
    )
    weigh = jnp.where(hit, gating[:, :, None], 0.0).reshape(requests, experts * CAP)
    slices = ranks // experts
    outgoing = jnp.broadcast_to(packed[:, None], (experts, slices, CAP, width)).reshape(
        ranks, CAP, width
    )
    arrived = lax.all_to_all(outgoing, "ranks", split_axis=0, concat_axis=0, tiled=True)
    count = arrived.shape[1]
    rows = arrived.reshape(-1, width)
    gate_val = jnp.dot(rows, expert_gate, preferred_element_type=jnp.float32)
    up_val = jnp.dot(rows, expert_up, preferred_element_type=jnp.float32)
    hidden = (jax.nn.silu(gate_val) * up_val).astype(jnp.bfloat16)
    partial_out = jnp.dot(hidden, expert_down, preferred_element_type=jnp.float32).reshape(
        ranks, count, width
    )
    returned = lax.all_to_all(
        partial_out.astype(jnp.bfloat16), "ranks", split_axis=0, concat_axis=0, tiled=True
    ).astype(partial_out.dtype)
    summed = jnp.sum(returned.reshape(experts, slices, CAP, width), axis=1)
    mine = lax.psum_scatter(
        summed.astype(jnp.bfloat16), "tp", scatter_dimension=2, tiled=True
    ).astype(jnp.float32)
    moe = jnp.dot(
        weigh,
        mine.reshape(experts * CAP, half),
        preferred_element_type=jnp.float32,
        precision=lax.Precision.HIGHEST,
    )
    layer_out = (middle_part.astype(jnp.float32) + moe).astype(jnp.bfloat16)
    return (layer_out, moved_k[None], moved_v[None])


def solution(mesh):
    return jax.shard_map(
        shards,
        mesh=mesh,
        in_specs=(
            P(("groups", "ranks"), "tp"),
            P(("groups", "ranks"), None, "tp"),
            P(("groups", "ranks"), None, "tp"),
            P(("groups", "ranks"), "tp"),
            P(("groups", "ranks"), "tp"),
            P(("groups", "ranks"), None),
            P(("groups", "ranks")),
            P(("groups", "ranks"), None),
            P(),
            P(),
            P(("groups", "ranks"), None),
            P(None, ("ranks", "tp")),
            P(None, ("ranks", "tp")),
            P(("ranks", "tp"), None),
        ),
        out_specs=(
            P(("groups", "ranks"), "tp"),
            P(("groups", "ranks"), None, "tp"),
            P(("groups", "ranks"), None, "tp"),
        ),
        check_vma=False,
    )
```

profile of v0, /device:TPU:1, one launch (start us, length us, event | category | flops | bytes accessed | tf_op | source)
XLA Modules:
  0.0 137.7 jit_solution(7937754278413270143)
XLA Ops:
  7.2 0.7 copy.49
  7.9 0.8 copy.48
  8.7 0.9 copy.50
  9.7 0.8 reshape.445
  10.5 0.6 gather_fusion.1
  11.1 2.8 %gather_fusion = bf16[64,16,512]{2,1,0:T(8,128)(2,1)} fusion(bf16[64,16,512]{2,1,0:T(8,128)(2,1)} %param.27, s32[1024]{0:T(1024)S(1)} %pad_clamp_fusion), kind=kCustom, calls=%fused_computation.2 | custom fusion | bytes 2097408 | tf_op jit(solution)/shard_map/gather | solution.py:24
  13.9 1.5 %bitcast_select_fusion.1 = (bf16[8,128,512]{2,1,0:T(8,128)(2,1)S(1)}, bf16[8,128,512]{2,1,0:T(8,128)(2,1)S(1)}) fusion(pred[8,128]{1,0:T(8,128)(4,1)S(1)} %get-tuple-element.77, pred[8,128]{1,0:T(8,128)(4,1)S(1)} %get-tuple-element.76, bf16[8,512]{1,0:T(8,128)(2,1)} %param.29, bf16[8,512]{1,0:T(8,128)(2,1)} %param.30, bf16[8,128,512]{2,1,0:T(8,128)(2,1)} %bitcast.81, ...), kind=kLoop, calls=%fused_computation.23 | loop fusion | flops 2097152 | bytes 4212736 | tf_op jit(solution)/shard_map/jit(_where)/select_n | solution.py:28
  15.5 3.2 %collective-permute-start.3 = (bf16[128,512]{1,0:T(8,128)(2,1)S(1)}, bf16[128,512]{1,0:T(8,128)(2,1)S(1)}, u32[]{:S(2)}, u32[]{:S(2)}) collective-permute-start(bf16[128,512]{1,0:T(8,128)(2,1)S(1)} %slice_bitcast_fusion.1), channel_id=1, source_target_pairs={{0,8},{2,10},{4,12},{6,14},{8,0},{10,2},{12,4},{14,6},{1,9},{3,11}... | collective-permute-start | bytes 393224 | tf_op jit(solution)/shard_map/ppermute | solution.py:16
  18.9 2.4 %collective-permute-start.2 = (bf16[3072]{0:T(1024)(128)(2,1)S(1)}, bf16[3072]{0:T(1024)(128)(2,1)S(1)}, u32[]{:S(2)}, u32[]{:S(2)}) collective-permute-start(bf16[3072]{0:T(1024)(128)(2,1)S(1)} %slice_reduce_fusion.1), channel_id=1, source_target_pairs={{0,8},{2,10},{4,12},{6,14},{8,0},{10,2},{12,4},{14,6},{1,9},{3,11}... | collective-permute-start | bytes 18440 | tf_op jit(solution)/shard_map/ppermute | solution.py:16
  21.5 2.4 %collective-permute-start = (bf16[6144]{0:T(1024)(128)(2,1)S(1)}, bf16[6144]{0:T(1024)(128)(2,1)S(1)}, u32[]{:S(2)}, u32[]{:S(2)}) collective-permute-start(bf16[6144]{0:T(1024)(128)(2,1)S(1)} %slice_reduce_fusion), channel_id=1, source_target_pairs={{0,8},{2,10},{4,12},{6,14},{8,0},{10,2},{12,4},{14,6},{1,9},{3,11}... | collective-permute-start | bytes 36872 | tf_op jit(solution)/shard_map/ppermute | solution.py:16
  23.9 0.8 fusion.39
  24.7 0.7 convert_element_type.83
  25.9 0.6 convert_reduce_fusion
  27.4 3.9 %collective-permute-done = bf16[6144]{0:T(1024)(128)(2,1)S(1)} collective-permute-done((bf16[6144]{0:T(1024)(128)(2,1)S(1)}, bf16[6144]{0:T(1024)(128)(2,1)S(1)}, u32[]{:S(2)}, u32[]{:S(2)}) %collective-permute-start) | collective-permute-done | bytes 12320 | tf_op jit(solution)/shard_map/ppermute | solution.py:16
  31.3 0.3 scatter.16
  31.7 0.6 fusion.6
  32.5 0.6 constant_dynamic-update-slice_fusion
  33.2 1.8 %fusion.7 = f32[8,4,6,128]{3,2,1,0:T(8,128)S(1)} fusion(f32[8,4,6]{2,1,0:T(4,128)S(1)} %fusion.41, f32[8,4,6,128]{3,2,1,0:T(8,128)S(1)} %fusion.6, bf16[8,128,512]{2,1,0:T(8,128)(2,1)} %constant_dynamic-update-slice_fusion), kind=kOutput, calls=%fused_computation.17 | convolution fusion | flops 6414655 | bytes 1245952 | tf_op jit(solution)/shard_map/rgqp,rpgd->rgqd/dot_general | solution.py:57
  35.1 2.7 %all_gather.3 = bf16[8,6144]{1,0:T(8,128)(2,1)S(1)} all-gather(bf16[8,3072]{1,0:T(8,128)(2,1)S(1)} %add_convert_fusion), channel_id=1, replica_groups=mesh['groups'=2,'ranks'=8,'tp'=2] {'tp'}, dimensions={1}, use_global_device_ids=true | all-gather | bytes 147456 | tf_op jit(solution)/shard_map/all_gather | solution.py:100
  38.4 24.5 %all_to_all.10 = bf16[8,6,6144]{2,1,0:T(8,128)(2,1)S(1)} all-to-all(bf16[8,6,6144]{2,1,0:T(8,128)(2,1)S(1)} %bitcast.82), channel_id=1, replica_groups=mesh['groups'=2,'ranks'=8,'tp'=2] {'ranks'}, dimensions={0} | all-to-all | bytes 1179648 | tf_op jit(solution)/shard_map/all_to_all | solution.py:134
  63.1 10.5 %fusion.42 = f32[48,2048]{1,0:T(8,128)S(1)} fusion(bf16[48,6144]{1,0:T(8,128)(2,1)S(1)} %reshape.453, bf16[6144,2048]{1,0:T(8,128)(2,1)} %param.37), kind=kOutput, calls=%fused_computation.90 | convolution fusion | flops 1207959552 | bytes 26148864 | tf_op jit(solution)/shard_map/dot_general | solution.py:137
  73.6 19.9 %convolution_convert_fusion = bf16[48,6144]{1,0:T(8,128)(2,1)S(1)} fusion(bf16[2048,6144]{1,0:T(8,128)(2,1)} %param.39, bf16[48,6144]{1,0:T(8,128)(2,1)S(1)} %reshape.453, bf16[6144,2048]{1,0:T(8,128)(2,1)} %param.38, f32[48,2048]{1,0:T(8,128)S(1)} %fusion.42), kind=kOutput, calls=%fused_computation.5 | convolution fusion | flops 2416803840 | bytes 51904512 | tf_op jit(solution)/shard_map/dot_general | solution.py:140
  93.6 1.1 convert_element_type.88
  94.6 4.1 %all-to-all-start.1 = ((bf16[8,6,6144]{2,1,0:T(8,128)(2,1)}), bf16[8,6,6144]{2,1,0:T(8,128)(2,1)S(1)}, u32[]{:S(2)}, u32[]{:S(2)}) async-start(bf16[8,6,6144]{2,1,0:T(8,128)(2,1)} %convert_element_type.88), calls=%async_computation.1 | async-start | bytes 1572864 | tf_op jit(solution)/shard_map/all_to_all | solution.py:143
  99.1 0.7 gather_fusion.2
  99.8 0.7 gather_fusion.3
  100.4 17.2 %all-to-all-done.1 = bf16[8,6,6144]{2,1,0:T(8,128)(2,1)S(1)} async-done(((bf16[8,6,6144]{2,1,0:T(8,128)(2,1)}), bf16[8,6,6144]{2,1,0:T(8,128)(2,1)S(1)}, u32[]{:S(2)}, u32[]{:S(2)}) %all-to-all-start.1) | async-done | bytes 589856 | tf_op jit(solution)/shard_map/all_to_all | solution.py:143
  117.6 0.9 bitcast_reduce_fusion
  118.7 8.7 %reduce-scatter.2.cloned.1.call-done = bf16[4,6,3072]{2,1,0:T(8,128)(2,1)} async-done(((bf16[4,6,6144]{2,1,0:T(8,128)(2,1)}), bf16[4,6,3072]{2,1,0:T(8,128)(2,1)}) %reduce-scatter.2.cloned.1.call-update) | async-done | bytes 147472 | tf_op jit(solution)/shard_map/reduce_scatter | solution.py:147
  127.5 2.1 %fusion.2 = bf16[8,3072]{1,0:T(8,128)(2,1)} fusion(bf16[4,6,3072]{2,1,0:T(8,128)(2,1)} %reduce-scatter.2.cloned.1.call-done, bf16[8,3072]{1,0:T(8,128)(2,1)S(1)} %add_convert_fusion, f32[8,4,6]{2,1,0:T(4,128)S(1)} %fusion.25), kind=kOutput, calls=%fused_computation.9 | convolution fusion | flops 7151616 | bytes 246528 | tf_op jit(solution)/shard_map/dot_general | solution.py:150
  129.5 0.7 copy.51
  130.2 0.7 copy.52
  (54 shorter events, 2.8 us)
Async XLA Ops:
  7.2 3.3 %copy-start = (bf16[64,16,512]{2,1,0:T(8,128)(2,1)S(1)}, bf16[64,16,512]{2,1,0:T(8,128)(2,1)}, u32[]{:S(2)}) copy-start(bf16[64,16,512]{2,1,0:T(8,128)(2,1)} %param.28) | copy-start | bytes 3145732
  15.5 5.8 %copy-start.1 = (bf16[8,128,512]{2,1,0:T(8,128)(2,1)}, bf16[8,128,512]{2,1,0:T(8,128)(2,1)S(1)}, u32[]{:S(2)}) copy-start(bf16[8,128,512]{2,1,0:T(8,128)(2,1)S(1)} %get-tuple-element.67) | copy-start | bytes 3145732
  15.5 16.1 %collective-permute-start.3 = (bf16[128,512]{1,0:T(8,128)(2,1)S(1)}, bf16[128,512]{1,0:T(8,128)(2,1)S(1)}, u32[]{:S(2)}, u32[]{:S(2)}) collective-permute-start(bf16[128,512]{1,0:T(8,128)(2,1)S(1)} %slice_bitcast_fusion.1), channel_id=1, source_target_pairs={{0,8},{2,10},{4,12},{6,14},{8,0},{10,2},{12,4},{14,6},{1,9},{3,11}... | collective-permute-start | bytes 393224 | tf_op jit(solution)/shard_map/ppermute | solution.py:16
  18.8 7.1 %collective-permute-start.1 = (bf16[128]{0:T(256)(128)(2,1)S(1)}, bf16[128]{0:T(256)(128)(2,1)S(1)}, u32[]{:S(2)}, u32[]{:S(2)}) collective-permute-start(bf16[128]{0:T(256)(128)(2,1)S(1)} %compare_convert_fusion), channel_id=1, source_target_pairs={{0,8},{2,10},{4,12},{6,14},{8,0},{10,2},{12,4},{14,6},{1,9},{3,11}... | collective-permute-start | bytes 776 | tf_op jit(solution)/shard_map/ppermute | solution.py:16
  18.9 8.3 %collective-permute-start.2 = (bf16[3072]{0:T(1024)(128)(2,1)S(1)}, bf16[3072]{0:T(1024)(128)(2,1)S(1)}, u32[]{:S(2)}, u32[]{:S(2)}) collective-permute-start(bf16[3072]{0:T(1024)(128)(2,1)S(1)} %slice_reduce_fusion.1), channel_id=1, source_target_pairs={{0,8},{2,10},{4,12},{6,14},{8,0},{10,2},{12,4},{14,6},{1,9},{3,11}... | collective-permute-start | bytes 18440 | tf_op jit(solution)/shard_map/ppermute | solution.py:16
  21.3 11.2 %collective-permute-start.4 = (bf16[128,512]{1,0:T(8,128)(2,1)S(1)}, bf16[128,512]{1,0:T(8,128)(2,1)S(1)}, u32[]{:S(2)}, u32[]{:S(2)}) collective-permute-start(bf16[128,512]{1,0:T(8,128)(2,1)S(1)} %slice_bitcast_fusion), channel_id=1, source_target_pairs={{0,8},{2,10},{4,12},{6,14},{8,0},{10,2},{12,4},{14,6},{1,9},{3,11}... | collective-permute-start | bytes 393224 | tf_op jit(solution)/shard_map/ppermute | solution.py:16
  21.5 9.8 %collective-permute-start = (bf16[6144]{0:T(1024)(128)(2,1)S(1)}, bf16[6144]{0:T(1024)(128)(2,1)S(1)}, u32[]{:S(2)}, u32[]{:S(2)}) collective-permute-start(bf16[6144]{0:T(1024)(128)(2,1)S(1)} %slice_reduce_fusion), channel_id=1, source_target_pairs={{0,8},{2,10},{4,12},{6,14},{8,0},{10,2},{12,4},{14,6},{1,9},{3,11}... | collective-permute-start | bytes 36872 | tf_op jit(solution)/shard_map/ppermute | solution.py:16
  73.6 25.3 %copy-start.3 = (bf16[6144,4]{0,1:T(4,128)(2,1)S(1)}, bf16[6144,4]{0,1:T(4,128)(2,1)}, u32[]{:S(2)}) copy-start(bf16[6144,4]{0,1:T(4,128)(2,1)} %param.35) | copy-start | bytes 147460
  73.6 44.9 %copy-start.2 = (s32[8,2]{0,1:T(2,128)S(1)}, s32[8,2]{0,1:T(2,128)}, u32[]{:S(2)}) copy-start(s32[8,2]{0,1:T(2,128)} %param.36) | copy-start | bytes 196
  94.6 22.9 %all-to-all-start.1 = ((bf16[8,6,6144]{2,1,0:T(8,128)(2,1)}), bf16[8,6,6144]{2,1,0:T(8,128)(2,1)S(1)}, u32[]{:S(2)}, u32[]{:S(2)}) async-start(bf16[8,6,6144]{2,1,0:T(8,128)(2,1)} %convert_element_type.88), calls=%async_computation.1 | async-start | bytes 1572864 | tf_op jit(solution)/shard_map/all_to_all | solution.py:143
  98.8 28.7 %reduce-scatter.2.cloned.1.call-start = ((), (), s32[]{:S(2)}) async-start(), calls=%async_computation.3 | async-start | bytes 589824 | tf_op jit(solution)/shard_map/reduce_scatter | solution.py:147
Sparse Core Ops, SparseCore 0:
  118.7 8.7 reduce-scatter.1
where the time goes:
time: 138 us
  matrix products  35.4 us (26%)
  waiting for transfers between devices  29.8 us (22%)
  blocking collectives  27.2 us (20%)
  between operations  14.9 us (11%)
  local copies, waits for them, and re-layouts  12.6 us (9%)
  starting transfers between devices  12.4 us (9%)
  other arithmetic  5.4 us (4%)
    all_to_all x1, blocking collectives, shards(): lax.all_to_all(outgoing, 'ranks', split_axis=0, concat_axis=0, tiled=True)  24.5 us
    dot_general x1, matrix products, shards(): jnp.dot(hidden, expert_down, preferred_element_type=jnp.float32)  19.9 us
    all_to_all x1, waiting for transfers between devices, shards(): lax.all_to_all(partial_out.astype(jnp.bfloat16), 'ranks', split_axis=0, c...  17.2 us
    dot_general x1, matrix products, shards(): gate_val = jnp.dot(rows, expert_gate, preferred_element_type=jnp.float32)  10.5 us
    reduce_scatter x1, waiting for transfers between devices, shards(): lax.psum_scatter(summed.astype(jnp.bfloat16), 'tp', scatter_dimension=2,...  8.73 us
    ppermute x5, starting transfers between devices, shifted(): return lax.ppermute(value, axis, pairs)  8.19 us
    all_to_all x1, starting transfers between devices, shards(): lax.all_to_all(partial_out.astype(jnp.bfloat16), 'ranks', split_axis=0, c...  4.13 us
    ppermute x5, waiting for transfers between devices, shifted(): return lax.ppermute(value, axis, pairs)  3.92 us
  transfers between devices with their start and end apart: 7, of which 3 were waited for; matrix products, arithmetic and copies ran while one was open for 4% of the time, Pallas kernels for 0%

commit v1 on v0

v1 whole, which is shorter than its diff:
```python
import functools

import jax
import jax.numpy as jnp
from jax import lax
from jax.experimental import pallas as pl
from jax.experimental.pallas import tpu as pltpu
from jax.sharding import PartitionSpec as P

HD = 128
EPSILON = 1e-05
F32 = jnp.float32
BF16 = jnp.bfloat16
MESH = pl.DeviceIdType.MESH
SLOTS = 8


def iota(shape, axis):
    return lax.broadcasted_iota(jnp.int32, shape, axis)


def kernel(
    sizes,
    table, lens, q_ref, pk_ref, pv_ref, fk_ref, fv_ref, stream_ref, gain_ref,
    router_ref, ext_ref, gate_hbm, up_hbm, down_hbm,
    out_ref, mk_ref, mv_ref,
    wbuf, kv0, attn_s, tok_a, tok_b, normed_s, e1_s, e2_s, hid_s,
    sib_s, sib_r, ret_s, ret_r,
    w_sem, d_sem, bar_a_send, bar_a_recv, tok_b_send, tok_b_recv,
    sib_send, sib_recv, ret_send, ret_recv, mv_send, mv_recv,
):
    ranks, experts, requests, ctx, blk, groups, share, depth, hidden, fc, slots = sizes
    half = depth // 2
    quarter = half // 2
    me = lax.axis_index("ranks")
    tp = lax.axis_index("tp")
    other = 1 - tp
    partner = lax.rem(me + ranks // 2, ranks)
    tokens = ranks * requests
    chunks = hidden // fc
    stacked = depth // hidden
    cols = depth // fc
    nj = cols // 2
    nm = nj // 2

    barrier = pltpu.get_barrier_semaphore()

    def greet(d, _):
        pl.semaphore_signal(
            barrier, inc=1, device_id={"ranks": lax.rem(me + d, ranks)}, device_id_type=MESH
        )
        return 0

    lax.fori_loop(1, ranks, greet, 0)
    pl.semaphore_signal(barrier, inc=1, device_id={"tp": other}, device_id_type=MESH)

    def gu_copy(u):
        src = gate_hbm if u % 2 == 0 else up_hbm
        return pltpu.make_async_copy(
            src.at[:, pl.ds((u // 2) * fc, fc)], wbuf.at[u % slots], w_sem.at[u]
        )

    def d_copy(n):
        at = (
            (other * nj + n) if n < nj else (tp * nj + (n - nj))
        )
        u = 2 * chunks + n // stacked
        return pltpu.make_async_copy(
            down_hbm.at[:, pl.ds(pl.multiple_of(at * fc, fc), fc)],
            wbuf.at[u % slots, pl.ds((n % stacked) * hidden, hidden)],
            d_sem.at[n],
        )

    def start_unit(u):
        if u < 2 * chunks:
            gu_copy(u).start()
        else:
            first = (u - 2 * chunks) * stacked
            for n in range(first, min(first + stacked, cols)):
                d_copy(n).start()

    units = 2 * chunks + -(-cols // stacked)
    for u in range(min(slots, units)):
        start_unit(u)
    started = min(slots, units)

    def attend(i, _):
        limit = lens[i]
        pos = iota((ctx, groups * HD), 0)
        row = iota((requests, groups * HD), 0)

        def logical(pool, fresh):
            x = jnp.concatenate(
                [pool[table[i, j]].astype(F32) for j in range(ctx // blk)], axis=0
            )
            new = jnp.sum(jnp.where(row == i, fresh[...].astype(F32), 0.0), axis=0, keepdims=True)
            return jnp.where(pos < limit, x, jnp.where(pos == limit, new, 0.0)).astype(BF16)

        keys = logical(pk_ref, fk_ref)
        values = logical(pv_ref, fv_ref)

        @pl.when(i == 0)
        def _():
            kv0[0] = keys
            kv0[1] = values

        for g in range(groups):
            q = q_ref[i, g]
            s = lax.dot_general(
                q, keys[:, g * HD:(g + 1) * HD], (((1,), (1,)), ((), ())),
                preferred_element_type=F32,
            ) * HD ** (-0.5)
            s = jnp.where(iota(s.shape, 1) <= limit, s, -1e30)
            p = jnp.exp(s - jnp.max(s, axis=1, keepdims=True))
            p = (p / jnp.sum(p, axis=1, keepdims=True)).astype(BF16)
            o = jnp.dot(p, values[:, g * HD:(g + 1) * HD], preferred_element_type=F32)
            for h in range(share):
                attn_s[g * share + h, pl.ds(i, 1), :] = o[h:h + 1, :]
        return 0

    lax.fori_loop(0, requests, attend, 0)

    own = stream_ref[:, pl.ds(pl.multiple_of(tp * half, half), half)].astype(F32)
    attn = jnp.concatenate([attn_s[h] for h in range(groups * share)], axis=1)
    mid = own + attn.astype(BF16).astype(F32)
    tok_a[me, :, :quarter] = jnp.concatenate(
        [mid[:, :quarter], mid[:, quarter:]], axis=0
    ).astype(BF16)
    tok_a[me, :, quarter:] = ext_ref[...]

    pl.semaphore_wait(barrier, ranks)

    def a_copy(p, src):
        return pltpu.make_async_remote_copy(
            src_ref=tok_a.at[src], dst_ref=tok_a.at[src],
            send_sem=bar_a_send.at[p], recv_sem=bar_a_recv.at[src],
            device_id={"ranks": p}, device_id_type=MESH,
        )

    def b_copy(r):
        return pltpu.make_async_remote_copy(
            src_ref=tok_a.at[r], dst_ref=tok_b.at[r],
            send_sem=tok_b_send.at[r], recv_sem=tok_b_recv.at[r],
            device_id={"tp": other}, device_id_type=MESH,
        )

    def send_a(d, _):
        a_copy(lax.rem(me + d, ranks), me).start()
        return 0

    lax.fori_loop(1, ranks, send_a, 0)
    b_copy(me).start()

    def forward(d, _):
        r = lax.rem(me + ranks - d, ranks)
        a_copy(r, r).wait_recv()
        b_copy(r).start()
        return 0

    lax.fori_loop(1, ranks, forward, 0)

    moved = [
        pltpu.make_async_remote_copy(
            src_ref=kv0.at[n], dst_ref=ref.at[0],
            send_sem=mv_send.at[n], recv_sem=mv_recv.at[n],
            device_id={"ranks": partner}, device_id_type=MESH,
        )
        for n, ref in enumerate((mk_ref, mv_ref))
    ]

    def wait_b(r, _):
        b_copy(r).wait_recv()
        return 0

    lax.fori_loop(0, ranks, wait_b, 0)
    for copy in moved:
        copy.start()

    def served(tok, r):
        swap = lax.rem(iota((2 * requests, quarter), 0), requests) == 0
        far = tok[lax.rem(r + ranks // 2, ranks), :, :quarter].astype(F32)
        x = jnp.where(swap, far, tok[r, :, :quarter].astype(F32))
        return x[:requests], x[requests:]

    at_a = pl.multiple_of(tp * half, half)
    at_b = pl.multiple_of(other * half, half)
    places = (
        at_a, pl.multiple_of(at_a + quarter, quarter),
        at_b, pl.multiple_of(at_b + quarter, quarter),
    )

    def normalise(m, _):
        rows = []
        for r in (2 * m, 2 * m + 1):
            parts = served(tok_a, r) + served(tok_b, r)
            square = sum(jnp.sum(x * x, axis=1, keepdims=True) for x in parts)
            scale = lax.rsqrt(square / depth + EPSILON)
            rows.append([x * scale for x in parts])
            ext = tok_a[r, :, quarter:].astype(F32)
            base = pl.multiple_of(r * requests, requests)
            e1_s[pl.ds(base, requests), :] = ext[:requests]
            e2_s[pl.ds(base, requests), :] = ext[requests:]
        span = pl.ds(pl.multiple_of(m * 2 * requests, 2 * requests), 2 * requests)
        for n, place in enumerate(places):
            x = jnp.concatenate([rows[0][n], rows[1][n]], axis=0)
            gain = gain_ref[:, pl.ds(place, quarter)].astype(F32)
            normed_s[span, pl.ds(place, quarter)] = (x * gain).astype(BF16)
        return 0

    lax.fori_loop(0, ranks // 2, normalise, 0)

    logits = lax.dot_general(
        normed_s[...], router_ref[...], (((1,), (1,)), ((), ())), preferred_element_type=F32
    )
    lane = iota(logits.shape, 1).astype(F32)
    e1, e2 = e1_s[:, :1], e2_s[:, :1]
    first = jnp.sum(jnp.where(lane == e1, logits, 0.0), axis=1, keepdims=True)
    second = jnp.sum(jnp.where(lane == e2, logits, 0.0), axis=1, keepdims=True)
    share1 = jax.nn.sigmoid(first - second)
    mine = (me // (ranks // experts)).astype(F32)
    weight = jnp.where(e1 == mine, share1, 0.0) + jnp.where(e2 == mine, 1.0 - share1, 0.0)

    kstep = depth // 3
    for c in range(chunks):
        gu_copy(2 * c).wait()
        gu_copy(2 * c + 1).wait()
        gs, us = (2 * c) % slots, (2 * c + 1) % slots

        def step(k, acc):
            span = pl.ds(pl.multiple_of(k * kstep, kstep), kstep)
            x = normed_s[:, span]
            return (
                acc[0] + jnp.dot(x, wbuf[gs, span, :], preferred_element_type=F32),
                acc[1] + jnp.dot(x, wbuf[us, span, :], preferred_element_type=F32),
            )

        zero = jnp.zeros((tokens, fc), F32)
        g, u = lax.fori_loop(0, 3, step, (zero, zero))
        hid_s[:, c * fc:(c + 1) * fc] = (jax.nn.silu(g) * u).astype(BF16)
        for _ in range(2):
            if started < units:
                start_unit(started)
                started += 1
    assert started == units

    def sib_copy(j):
        return pltpu.make_async_remote_copy(
            src_ref=sib_s.at[j], dst_ref=sib_r.at[j],
            send_sem=sib_send.at[j], recv_sem=sib_recv.at[j],
            device_id={"tp": other}, device_id_type=MESH,
        )

    def ret_copy(m, p, src):
        return pltpu.make_async_remote_copy(
            src_ref=ret_s.at[m, p], dst_ref=ret_r.at[m, src],
            send_sem=ret_send.at[m, p], recv_sem=ret_recv.at[m, src],
            device_id={"ranks": p}, device_id_type=MESH,
        )

    held = None
    for n in range(cols):
        d_copy(n).wait()
        slot = (2 * chunks + n // stacked) % slots
        w = wbuf[slot, (n % stacked) * hidden:(n % stacked + 1) * hidden, :]
        y = jnp.dot(hid_s[...], w, preferred_element_type=F32) * weight
        if n < nj:
            sib_s[n] = y.astype(BF16)
            sib_copy(n).start()
            continue
        j = n - nj
        sib_copy(j).wait_recv()
        y = (y + sib_r[j].astype(F32)).reshape(ranks, requests, fc)
        if j % 2 == 0:
            held = y
            continue
        m = j // 2
        ret_s[m] = jnp.concatenate([held, y], axis=1).astype(BF16)

        def send_ret(d, _, m=m):
            p = lax.rem(me + d, ranks)
            ret_copy(m, p, me).start()
            return 0

        lax.fori_loop(1, ranks, send_ret, 0)

    lo, hi = served(tok_a, me)
    mid_now = jnp.concatenate([lo, hi], axis=1)
    for m in range(nm):
        def gather(d, total, m=m):
            r = lax.rem(me + ranks - d, ranks)
            ret_copy(m, r, r).wait_recv()
            return total + ret_r[m, r].astype(F32)

        total = lax.fori_loop(1, ranks, gather, ret_s[m, me].astype(F32))
        for b in range(2):
            span = slice((2 * m + b) * fc, (2 * m + b + 1) * fc)
            out_ref[:, span] = (
                mid_now[:, span] + total[b * requests:(b + 1) * requests]
            ).astype(BF16)

    def drain(d, _):
        p = lax.rem(me + d, ranks)
        a_copy(p, me).wait_send()
        for m in range(nm):
            ret_copy(m, p, me).wait_send()
        return 0

    lax.fori_loop(1, ranks, drain, 0)

    def drain_b(r, _):
        b_copy(r).wait_send()
        return 0

    lax.fori_loop(0, ranks, drain_b, 0)
    for j in range(nj):
        sib_copy(j).wait_send()
    for copy in moved:
        copy.wait()


def shards(
    ranks, queries, cache_keys, cache_values, fresh_keys, fresh_values, block_table, lengths,
    stream, norm_gain, router, routes, expert_gate, expert_up, expert_down,
):
    requests, half = queries.shape
    depth = 2 * half
    experts = router.shape[1]
    blk, width = cache_keys.shape[1:]
    ctx = block_table.shape[1] * blk
    groups = width // HD
    share = half // HD // groups
    hidden = expert_gate.shape[1]
    fc = min(512, hidden)
    chunks = hidden // fc
    cols = depth // fc
    nj = cols // 2
    nm = nj // 2
    quarter = half // 2
    tokens = ranks * requests
    units = 2 * chunks + -(-cols // (depth // hidden))
    slots = min(SLOTS, units)
    q = jnp.pad(
        queries.reshape(requests, groups, share, HD), ((0, 0), (0, 0), (0, 16 - share), (0, 0))
    )
    router_t = jnp.pad(router.T, ((0, 16 - experts), (0, 0)))
    ext = jnp.broadcast_to(routes.T.reshape(2 * requests, 1), (2 * requests, 128)).astype(BF16)
    sizes = (ranks, experts, requests, ctx, blk, groups, share, depth, hidden, fc, slots)
    vmem = pl.BlockSpec(memory_space=pltpu.VMEM)
    smem = pl.BlockSpec(memory_space=pltpu.SMEM)
    hbm = pl.BlockSpec(memory_space=pl.ANY)
    dma = pltpu.SemaphoreType.DMA
    tok = quarter + 128
    moved = jax.ShapeDtypeStruct((1, ctx, width), BF16)
    return pl.pallas_call(
        functools.partial(kernel, sizes),
        out_shape=(jax.ShapeDtypeStruct((requests, half), BF16), moved, moved),
        in_specs=[smem, smem] + [vmem] * 9 + [hbm] * 3,
        out_specs=(vmem, hbm, hbm),
        scratch_shapes=[
            pltpu.VMEM((slots, depth, fc), BF16),
            pltpu.VMEM((2, ctx, width), BF16),
            pltpu.VMEM((half // HD, requests, HD), F32),
            pltpu.VMEM((ranks, 2 * requests, tok), BF16),
            pltpu.VMEM((ranks, 2 * requests, tok), BF16),
            pltpu.VMEM((tokens, depth), BF16),
            pltpu.VMEM((tokens, 128), F32),
            pltpu.VMEM((tokens, 128), F32),
            pltpu.VMEM((tokens, hidden), BF16),
            pltpu.VMEM((nj, tokens, fc), BF16),
            pltpu.VMEM((nj, tokens, fc), BF16),
            pltpu.VMEM((nm, ranks, 2 * requests, fc), BF16),
            pltpu.VMEM((nm, ranks, 2 * requests, fc), BF16),
            dma((2 * chunks,)),
            dma((cols,)),
            dma((ranks,)),
            dma((ranks,)),
            dma((ranks,)),
            dma((ranks,)),
            dma((nj,)),
            dma((nj,)),
            dma((nm, ranks)),
            dma((nm, ranks)),
            dma((2,)),
            dma((2,)),
        ],
        compiler_params=pltpu.CompilerParams(
            collective_id=0, has_side_effects=True, vmem_limit_bytes=62 * 1024 * 1024
        ),
    )(
        block_table, lengths, q, cache_keys, cache_values, fresh_keys, fresh_values, stream,
        norm_gain.reshape(1, depth), router_t, ext, expert_gate, expert_up, expert_down,
    )


def solution(mesh):
    rows = ("groups", "ranks")
    return jax.shard_map(
        functools.partial(shards, mesh.shape["ranks"]),
        mesh=mesh,
        in_specs=(
            P(rows, "tp"), P(rows, None, "tp"), P(rows, None, "tp"), P(rows, "tp"),
            P(rows, "tp"), P(rows, None), P(rows), P(rows, None), P(), P(), P(rows, None),
            P(None, ("ranks", "tp")), P(None, ("ranks", "tp")), P(("ranks", "tp"), None),
        ),
        out_specs=(P(rows, "tp"), P(rows, None, "tp"), P(rows, None, "tp")),
        check_vma=False,
    )
```

time: 138 us -> 64.7 us (0.47)
  Pallas kernels: 0 us -> 53.4 us
  matrix products: 35.4 us -> 0 us
  waiting for transfers between devices: 29.8 us -> 0 us
  blocking collectives: 27.2 us -> 0 us
  between operations: 14.9 us -> 0.65 us
  starting transfers between devices: 12.4 us -> 0 us
  other arithmetic: 5.4 us -> 0.68 us
  local copies, waits for them, and re-layouts: 12.6 us -> 9.62 us
    pallas_call x0 -> x1, Pallas kernels: none -> 53.4 us  [shards(): pl.pallas_call(functools.partial(kernel, sizes), out_shape=(jax.ShapeDtyp...]
    dot_general x7 -> x0, matrix products: 35.4 us -> none  [the longest x1 19.9 us: shards(): jnp.dot(hidden, expert_down, preferred_element_type=jnp.float32)]
    all_to_all x1 -> x0, blocking collectives: 24.5 us -> none  [shards(): lax.all_to_all(outgoing, 'ranks', split_axis=0, concat_axis=0, tiled=True)]
    all_to_all x1 -> x0, waiting for transfers between devices: 17.2 us -> none  [shards(): lax.all_to_all(partial_out.astype(jnp.bfloat16), 'ranks', split_axis=0, c...]
    reduce_scatter x1 -> x0, waiting for transfers between devices: 8.73 us -> none  [shards(): lax.psum_scatter(summed.astype(jnp.bfloat16), 'tp', scatter_dimension=2,...]
    ppermute x5 -> x0, starting transfers between devices: 8.19 us -> none  [shifted(): return lax.ppermute(value, axis, pairs)]
    gather x4 -> x0, local copies, waits for them, and re-layouts: 4.77 us -> none  [the longest x1 2.83 us: logical_cache(): keys = pool_keys[flat].reshape(requests, context, width)]
    all_to_all x1 -> x0, starting transfers between devices: 4.13 us -> none  [shards(): lax.all_to_all(partial_out.astype(jnp.bfloat16), 'ranks', split_axis=0, c...]
  transfers between devices with their start and end apart: 7 -> 0, of which waited for: 3 -> 0; matrix products, arithmetic and copies ran while one was open for 4% -> 0% of each run, Pallas kernels for 0% -> 0%
where the time goes in v1:
time: 64.7 us; the launch traced here: 64.3 us
  Pallas kernels  53.4 us (83%)
  local copies, waits for them, and re-layouts  9.62 us (15%)
  other arithmetic  0.68 us (1%)
  between operations  0.65 us (1%)
    pallas_call x1, Pallas kernels, shards(): pl.pallas_call(functools.partial(kernel, sizes), out_shape=(jax.ShapeDtyp...  53.4 us
    unnamed x3, local copies, waits for them, and re-layouts  4.56 us
    pad x1, local copies, waits for them, and re-layouts, shards(): router_t = jnp.pad(router.T, ((0, 16 - experts), (0, 0)))  1.49 us
    reshape x1, local copies, waits for them, and re-layouts, shards(): norm_gain.reshape(1, depth)  1.33 us

profile of v1, /device:TPU:1, one launch (start us, length us, event | category | flops | bytes accessed | tf_op | source)
XLA Modules:
  0.0 64.3 jit_solution(3017425811733101098)
XLA Ops:
  0.6 0.7 %convert_bitcast_fusion = bf16[2,8]{1,0:T(2,128)(2,1)S(1)} fusion(s32[8,2]{0,1:T(2,128)} %param.24), kind=kLoop, calls=%fused_computation | loop fusion | flops 16 | bytes 96 | tf_op jit(solution)/shard_map/convert_element_type | solution.py:346
  1.3 0.1 convert_element_type.13
  1.4 0.7 %broadcast_in_dim.2.ext_ref = bf16[16,128]{1,0:T(8,128)(2,1)} broadcast(bf16[16]{0:T(256)(128)(2,1)S(1)} %convert_element_type.13), dimensions={0} | broadcast | bytes 4128 | tf_op jit(solution)/shard_map/broadcast_in_dim | solution.py:346
  2.1 1.3 %reshape.16.gain_ref = bf16[1,6144]{1,0:T(2,128)(2,1)} reshape(bf16[6144]{0:T(1024)(128)(2,1)} %param.22) | data formatting | bytes 24576 | tf_op jit(solution)/shard_map/reshape | solution.py:391
  3.4 0.8 %copy.17 = bf16[8,4,6,128]{3,2,1,0:T(8,128)(2,1)S(1)} copy(bf16[8,4,6,128]{3,0,2,1:T(8,128)(2,1)} %bitcast.4) | data formatting | bytes 98304 | tf_op jit(solution)/shard_map/reshape | solution.py:343
  4.2 0.7 %pad.8.q_ref = bf16[8,4,16,128]{3,2,1,0:T(8,128)(2,1)} pad(bf16[8,4,6,128]{3,2,1,0:T(8,128)(2,1)S(1)} %copy.17, bf16[]{:T(256)} %constant.2.clone.1), padding=0_0x0_0x0_10x0_0 | pad | bytes 180226 | tf_op jit(solution)/shard_map/jit(_pad)/pad | solution.py:342
  4.9 1.5 %pad.9.router_ref = bf16[16,6144]{1,0:T(8,128)(2,1)} pad(bf16[4,6144]{1,0:T(4,128)(2,1)} %bitcast.5, bf16[]{:T(256)} %constant.2.clone.1), padding=0_12x0_0 | pad | bytes 245762 | tf_op jit(solution)/shard_map/jit(_pad)/pad | solution.py:345
  6.4 53.4 %shard_map.157 = (bf16[8,3072]{1,0:T(8,128)(2,1)}, bf16[1,128,512]{2,1,0:T(8,128)(2,1)}, bf16[1,128,512]{2,1,0:T(8,128)(2,1)}) custom-call(s32[8,8]{1,0:T(8,128)} %table.1, s32[8]{0:T(128)} %lens.1, bf16[8,4,16,128]{3,2,1,0:T(8,128)(2,1)} %pad.8.q_ref, bf16[64,16,512]{2,1,0:T(8,128)(2,1)} %pk_ref.1, bf16[64,16,512]{2,1,0:T(8,128)(2,1)} %pv_ref.1, ...), custom_call_target="tpu_custom_call" | custom-call | tf_op jit(solution)/shard_map/pallas_call | solution.py:354
  59.7 1.4 %copy.21 = bf16[8,3072]{1,0:T(8,128)(2,1)} copy(bf16[8,3072]{1,0:T(8,128)(2,1)} %get-tuple-element.6) | data formatting | bytes 98304
  61.2 1.6 %copy.22 = bf16[1,128,512]{2,1,0:T(8,128)(2,1)} copy(bf16[1,128,512]{2,1,0:T(8,128)(2,1)} %get-tuple-element.7) | data formatting | bytes 262144
  62.7 1.6 %copy.23 = bf16[1,128,512]{2,1,0:T(8,128)(2,1)} copy(bf16[1,128,512]{2,1,0:T(8,128)(2,1)} %get-tuple-element.8) | data formatting | bytes 262144

commit v2 on v1

--- a/solution.py
+++ b/solution.py
@@ -12,7 +12,7 @@
 F32 = jnp.float32
 BF16 = jnp.bfloat16
 MESH = pl.DeviceIdType.MESH
-SLOTS = 8
+SLOTS = 9
 
 
 def iota(shape, axis):
@@ -22,9 +22,9 @@
 def kernel(
     sizes,
     table, lens, q_ref, pk_ref, pv_ref, fk_ref, fv_ref, stream_ref, gain_ref,
-    router_ref, ext_ref, gate_hbm, up_hbm, down_hbm,
+    router_ref, routes, gate_hbm, up_hbm, down_hbm,
     out_ref, mk_ref, mv_ref,
-    wbuf, kv0, attn_s, tok_a, tok_b, normed_s, e1_s, e2_s, hid_s,
+    wbuf, kv0, q_s, gain_s, router_s, attn_s, tok_a, tok_b, normed_s, e1_s, e2_s, hid_s,
     sib_s, sib_r, ret_s, ret_r,
     w_sem, d_sem, bar_a_send, bar_a_recv, tok_b_send, tok_b_recv,
     sib_send, sib_recv, ret_send, ret_recv, mv_send, mv_recv,
@@ -84,6 +84,15 @@
         start_unit(u)
     started = min(slots, units)
 
+    q_s[...] = jnp.zeros_like(q_s)
+    for h in range(groups * share):
+        q_s[h // share, :, h % share, :] = q_ref[:, h * HD:(h + 1) * HD].astype(F32)
+    gains = gain_ref[...].astype(F32)
+    for k in range(depth // 128):
+        gain_s[:, k * 128:(k + 1) * 128] = gains[k:k + 1]
+    router_s[...] = jnp.zeros_like(router_s)
+    router_s[:experts] = router_ref[...].astype(F32)
+
     def attend(i, _):
         limit = lens[i]
         pos = iota((ctx, groups * HD), 0)
@@ -105,7 +114,7 @@
             kv0[1] = values
 
         for g in range(groups):
-            q = q_ref[i, g]
+            q = q_s[g, i].astype(BF16)
             s = lax.dot_general(
                 q, keys[:, g * HD:(g + 1) * HD], (((1,), (1,)), ((), ())),
                 preferred_element_type=F32,
@@ -118,7 +127,7 @@
                 attn_s[g * share + h, pl.ds(i, 1), :] = o[h:h + 1, :]
         return 0
 
-    lax.fori_loop(0, requests, attend, 0)
+    lax.fori_loop(0, requests, attend, 0, unroll=4)
 
     own = stream_ref[:, pl.ds(pl.multiple_of(tp * half, half), half)].astype(F32)
     attn = jnp.concatenate([attn_s[h] for h in range(groups * share)], axis=1)
@@ -126,14 +135,24 @@
     tok_a[me, :, :quarter] = jnp.concatenate(
         [mid[:, :quarter], mid[:, quarter:]], axis=0
     ).astype(BF16)
-    tok_a[me, :, quarter:] = ext_ref[...]
+    which = iota((2 * requests, 128), 0)
+    ext = jnp.zeros((2 * requests, 128), F32)
+    for t in range(requests):
+        for e in range(2):
+            ext = jnp.where(which == e * requests + t, routes[e, t].astype(F32), ext)
+    tok_a[me, :, quarter:] = ext.astype(BF16)
 
     pl.semaphore_wait(barrier, ranks)
 
-    def a_copy(p, src):
+    def mate_of(r):
+        return r + 1 - 2 * lax.rem(r, 2)
+
+    mate = mate_of(me)
+
+    def a_copy(p, src, s):
         return pltpu.make_async_remote_copy(
             src_ref=tok_a.at[src], dst_ref=tok_a.at[src],
-            send_sem=bar_a_send.at[p], recv_sem=bar_a_recv.at[src],
+            send_sem=bar_a_send.at[s], recv_sem=bar_a_recv.at[src],
             device_id={"ranks": p}, device_id_type=MESH,
         )
 
@@ -145,19 +164,32 @@
         )
 
     def send_a(d, _):
-        a_copy(lax.rem(me + d, ranks), me).start()
-        return 0
-
-    lax.fori_loop(1, ranks, send_a, 0)
+        p = lax.rem(me + 2 * d, ranks)
+        a_copy(p, me, p).start()
+        return 0
+
+    lax.fori_loop(1, ranks // 2, send_a, 0)
+    a_copy(mate, me, mate).start()
     b_copy(me).start()
+    a_copy(mate, mate, mate).wait_recv()
+    b_copy(mate).start()
 
     def forward(d, _):
-        r = lax.rem(me + ranks - d, ranks)
-        a_copy(r, r).wait_recv()
+        r = lax.rem(me + ranks - 2 * d, ranks)
+        a_copy(r, r, r).wait_recv()
+        a_copy(mate, r, mate_of(r)).start()
         b_copy(r).start()
         return 0
 
-    lax.fori_loop(1, ranks, forward, 0)
+    lax.fori_loop(1, ranks // 2, forward, 0)
+
+    def forward_mate(d, _):
+        r = mate_of(lax.rem(me + ranks - 2 * d, ranks))
+        a_copy(r, r, r).wait_recv()
+        b_copy(r).start()
+        return 0
+
+    lax.fori_loop(1, ranks // 2, forward_mate, 0)
 
     moved = [
         pltpu.make_async_remote_copy(
@@ -203,14 +235,14 @@
         span = pl.ds(pl.multiple_of(m * 2 * requests, 2 * requests), 2 * requests)
         for n, place in enumerate(places):
             x = jnp.concatenate([rows[0][n], rows[1][n]], axis=0)
-            gain = gain_ref[:, pl.ds(place, quarter)].astype(F32)
+            gain = gain_s[:, pl.ds(place, quarter)]
             normed_s[span, pl.ds(place, quarter)] = (x * gain).astype(BF16)
         return 0
 
     lax.fori_loop(0, ranks // 2, normalise, 0)
 
     logits = lax.dot_general(
-        normed_s[...], router_ref[...], (((1,), (1,)), ((), ())), preferred_element_type=F32
+        normed_s[...], router_s[...].astype(BF16), (((1,), (1,)), ((), ())), preferred_element_type=F32
     )
     lane = iota(logits.shape, 1).astype(F32)
     e1, e2 = e1_s[:, :1], e2_s[:, :1]
@@ -300,12 +332,20 @@
 
     def drain(d, _):
         p = lax.rem(me + d, ranks)
-        a_copy(p, me).wait_send()
         for m in range(nm):
             ret_copy(m, p, me).wait_send()
         return 0
 
     lax.fori_loop(1, ranks, drain, 0)
+
+    def drain_a(d, _):
+        p = lax.rem(me + 2 * d, ranks)
+        a_copy(p, me, p).wait_send()
+        a_copy(mate, p, mate_of(p)).wait_send()
+        return 0
+
+    lax.fori_loop(1, ranks // 2, drain_a, 0)
+    a_copy(mate, me, mate).wait_send()
 
     def drain_b(r, _):
         b_copy(r).wait_send()
@@ -315,6 +355,14 @@
     for j in range(nj):
         sib_copy(j).wait_send()
     for copy in moved:
+        copy.wait()
+
+
+def deliver(*refs):
+    copies = [pltpu.make_async_copy(refs[n], refs[3 + n], refs[6].at[n]) for n in range(3)]
+    for copy in copies:
+        copy.start()
+    for copy in copies:
         copy.wait()
 
 
@@ -339,11 +387,6 @@
     tokens = ranks * requests
     units = 2 * chunks + -(-cols // (depth // hidden))
     slots = min(SLOTS, units)
-    q = jnp.pad(
-        queries.reshape(requests, groups, share, HD), ((0, 0), (0, 0), (0, 16 - share), (0, 0))
-    )
-    router_t = jnp.pad(router.T, ((0, 16 - experts), (0, 0)))
-    ext = jnp.broadcast_to(routes.T.reshape(2 * requests, 1), (2 * requests, 128)).astype(BF16)
     sizes = (ranks, experts, requests, ctx, blk, groups, share, depth, hidden, fc, slots)
     vmem = pl.BlockSpec(memory_space=pltpu.VMEM)
     smem = pl.BlockSpec(memory_space=pltpu.SMEM)
@@ -351,14 +394,17 @@
     dma = pltpu.SemaphoreType.DMA
     tok = quarter + 128
     moved = jax.ShapeDtypeStruct((1, ctx, width), BF16)
-    return pl.pallas_call(
+    results = pl.pallas_call(
         functools.partial(kernel, sizes),
         out_shape=(jax.ShapeDtypeStruct((requests, half), BF16), moved, moved),
-        in_specs=[smem, smem] + [vmem] * 9 + [hbm] * 3,
+        in_specs=[smem, smem] + [vmem] * 8 + [smem] + [hbm] * 3,
         out_specs=(vmem, hbm, hbm),
         scratch_shapes=[
             pltpu.VMEM((slots, depth, fc), BF16),
             pltpu.VMEM((2, ctx, width), BF16),
+            pltpu.VMEM((groups, requests, 8 * -(-share // 8), HD), F32),
+            pltpu.VMEM((1, depth), F32),
+            pltpu.VMEM((8 * -(-experts // 8), depth), F32),
             pltpu.VMEM((half // HD, requests, HD), F32),
             pltpu.VMEM((ranks, 2 * requests, tok), BF16),
             pltpu.VMEM((ranks, 2 * requests, tok), BF16),
@@ -387,9 +433,17 @@
             collective_id=0, has_side_effects=True, vmem_limit_bytes=62 * 1024 * 1024
         ),
     )(
-        block_table, lengths, q, cache_keys, cache_values, fresh_keys, fresh_values, stream,
-        norm_gain.reshape(1, depth), router_t, ext, expert_gate, expert_up, expert_down,
+        block_table, lengths, queries, cache_keys, cache_values, fresh_keys, fresh_values, stream,
+        norm_gain.reshape(depth // 128, 128), router.T, routes.T,
+        expert_gate, expert_up, expert_down,
     )
+    return pl.pallas_call(
+        deliver,
+        out_shape=[jax.ShapeDtypeStruct(x.shape, x.dtype) for x in results],
+        in_specs=[hbm] * 3,
+        out_specs=[hbm] * 3,
+        scratch_shapes=[dma((3,))],
+    )(*results)
 
 
 def solution(mesh):

time: 64.7 us -> 64.6 us (level)
  Pallas kernels: 53.4 us -> 63.8 us
  local copies, waits for them, and re-layouts: 9.62 us -> 0 us
  other arithmetic: 0.68 us -> 0 us
    pallas_call x0 -> x1, Pallas kernels: none -> 10.6 us  [shards(): pl.pallas_call(deliver, out_shape=[jax.ShapeDtypeStruct(x.shape, x.dtype)...]
    unnamed x3 -> x0, local copies, waits for them, and re-layouts: 4.56 us -> none
    pad x2 -> x0, local copies, waits for them, and re-layouts: 2.17 us -> none  [the longest x1 1.49 us: shards(): router_t = jnp.pad(router.T, ((0, 16 - experts), (0, 0)))]
    reshape x2 -> x0, local copies, waits for them, and re-layouts: 2.14 us -> none  [the longest x1 1.33 us: shards(): norm_gain.reshape(1, depth)]
    convert_element_type x1 -> x0, other arithmetic: 0.68 us -> none  [shards(): jnp.broadcast_to(routes.T.reshape(2 * requests, 1), (2 * requests, 128))]
    broadcast_in_dim x1 -> x0, local copies, waits for them, and re-layouts: 0.67 us -> none  [shards(): jnp.broadcast_to(routes.T.reshape(2 * requests, 1), (2 * requests, 128))]
where the time goes in v2:
time: 64.6 us; the launch traced here: 64.5 us
  Pallas kernels  63.8 us (99%)
    pallas_call x1, Pallas kernels, shards(): pl.pallas_call(functools.partial(kernel, sizes), out_shape=(jax.ShapeDtyp...  53.3 us
    pallas_call x1, Pallas kernels, shards(): pl.pallas_call(deliver, out_shape=[jax.ShapeDtypeStruct(x.shape, x.dtype)...  10.6 us

profile of v2, /device:TPU:1, one launch (start us, length us, event | category | flops | bytes accessed | tf_op | source)
XLA Modules:
  0.0 64.5 jit_solution(18364150845481861094)
XLA Ops:
  0.6 53.3 %shard_map.157 = (bf16[8,3072]{1,0:T(8,128)(2,1)}, bf16[1,128,512]{2,1,0:T(8,128)(2,1)}, bf16[1,128,512]{2,1,0:T(8,128)(2,1)}) custom-call(s32[8,8]{1,0:T(8,128)} %table.1, s32[8]{0:T(128)} %lens.1, bf16[8,3072]{1,0:T(8,128)(2,1)} %q_ref.1, bf16[64,16,512]{2,1,0:T(8,128)(2,1)} %pk_ref.1, bf16[64,16,512]{2,1,0:T(8,128)(2,1)} %pv_ref.1, ...), custom_call_target="tpu_custom_call" | custom-call | tf_op jit(solution)/shard_map/pallas_call | solution.py:397
  53.9 10.6 %shard_map.158 = (bf16[8,3072]{1,0:T(8,128)(2,1)}, bf16[1,128,512]{2,1,0:T(8,128)(2,1)}, bf16[1,128,512]{2,1,0:T(8,128)(2,1)}) custom-call(bf16[8,3072]{1,0:T(8,128)(2,1)} %get-tuple-element.6.refs_0_, bf16[1,128,512]{2,1,0:T(8,128)(2,1)} %get-tuple-element.7.refs_1_, bf16[1,128,512]{2,1,0:T(8,128)(2,1)} %get-tuple-element.8.refs_2_), custom_call_target="tpu_custom_call" | custom-call | tf_op jit(solution)/shard_map/pallas_call | solution.py:440

commit v3 on v2

--- a/solution.py
+++ b/solution.py
@@ -440,7 +440,7 @@
     return pl.pallas_call(
         deliver,
         out_shape=[jax.ShapeDtypeStruct(x.shape, x.dtype) for x in results],
-        in_specs=[hbm] * 3,
+        in_specs=[vmem] * 3,
         out_specs=[hbm] * 3,
         scratch_shapes=[dma((3,))],
     )(*results)

time: 64.6 us -> 55.8 us (0.86)
  Pallas kernels: 63.8 us -> 55 us
    pallas_call x1, Pallas kernels: 10.6 us -> 1.73 us  [shards(): pl.pallas_call(deliver, out_shape=[jax.ShapeDtypeStruct(x.shape, x.dtype)...]
where the time goes in v3:
time: 55.8 us; the launch traced here: 55.7 us
  Pallas kernels  55 us (99%)
  between operations  0.64 us (1%)
    pallas_call x1, Pallas kernels, shards(): pl.pallas_call(functools.partial(kernel, sizes), out_shape=(jax.ShapeDtyp...  53.3 us
    pallas_call x1, Pallas kernels, shards(): pl.pallas_call(deliver, out_shape=[jax.ShapeDtypeStruct(x.shape, x.dtype)...  1.73 us

profile of v3, /device:TPU:1, one launch (start us, length us, event | category | flops | bytes accessed | tf_op | source)
XLA Modules:
  0.0 55.7 jit_solution(2545375894745724581)
XLA Ops:
  0.6 53.3 %shard_map.157 = (bf16[8,3072]{1,0:T(8,128)(2,1)}, bf16[1,128,512]{2,1,0:T(8,128)(2,1)}, bf16[1,128,512]{2,1,0:T(8,128)(2,1)}) custom-call(s32[8,8]{1,0:T(8,128)} %table.1, s32[8]{0:T(128)} %lens.1, bf16[8,3072]{1,0:T(8,128)(2,1)} %q_ref.1, bf16[64,16,512]{2,1,0:T(8,128)(2,1)} %pk_ref.1, bf16[64,16,512]{2,1,0:T(8,128)(2,1)} %pv_ref.1, ...), custom_call_target="tpu_custom_call" | custom-call | tf_op jit(solution)/shard_map/pallas_call | solution.py:397
  53.9 1.7 %shard_map.158 = (bf16[8,3072]{1,0:T(8,128)(2,1)}, bf16[1,128,512]{2,1,0:T(8,128)(2,1)}, bf16[1,128,512]{2,1,0:T(8,128)(2,1)}) custom-call(bf16[8,3072]{1,0:T(8,128)(2,1)} %get-tuple-element.6.refs_0_, bf16[1,128,512]{2,1,0:T(8,128)(2,1)} %get-tuple-element.7.refs_1_, bf16[1,128,512]{2,1,0:T(8,128)(2,1)} %get-tuple-element.8.refs_2_), custom_call_target="tpu_custom_call" | custom-call | tf_op jit(solution)/shard_map/pallas_call | solution.py:440

commit v4 on v3

--- a/solution.py
+++ b/solution.py
@@ -239,7 +239,7 @@
             normed_s[span, pl.ds(place, quarter)] = (x * gain).astype(BF16)
         return 0
 
-    lax.fori_loop(0, ranks // 2, normalise, 0)
+    lax.fori_loop(0, ranks // 2, normalise, 0, unroll=2)
 
     logits = lax.dot_general(
         normed_s[...], router_s[...].astype(BF16), (((1,), (1,)), ((), ())), preferred_element_type=F32
@@ -267,7 +267,7 @@
             )
 
         zero = jnp.zeros((tokens, fc), F32)
-        g, u = lax.fori_loop(0, 3, step, (zero, zero))
+        g, u = lax.fori_loop(0, 3, step, (zero, zero), unroll=True)
         hid_s[:, c * fc:(c + 1) * fc] = (jax.nn.silu(g) * u).astype(BF16)
         for _ in range(2):
             if started < units:

time: 55.8 us -> 54.9 us (0.984)
  Pallas kernels: 55 us -> 54.1 us
    pallas_call x1, Pallas kernels: 53.3 us -> 52.3 us  [shards(): pl.pallas_call(functools.partial(kernel, sizes), out_shape=(jax.ShapeDtyp...]
where the time goes in v4:
time: 54.9 us; the launch traced here: 54.7 us
  Pallas kernels  54.1 us (99%)
  between operations  0.64 us (1%)
    pallas_call x1, Pallas kernels, shards(): pl.pallas_call(functools.partial(kernel, sizes), out_shape=(jax.ShapeDtyp...  52.3 us
    pallas_call x1, Pallas kernels, shards(): pl.pallas_call(deliver, out_shape=[jax.ShapeDtypeStruct(x.shape, x.dtype)...  1.73 us

profile of v4, /device:TPU:1, one launch (start us, length us, event | category | flops | bytes accessed | tf_op | source)
XLA Modules:
  0.0 54.7 jit_solution(2428097350871997118)
XLA Ops:
  0.6 52.3 %shard_map.157 = (bf16[8,3072]{1,0:T(8,128)(2,1)}, bf16[1,128,512]{2,1,0:T(8,128)(2,1)}, bf16[1,128,512]{2,1,0:T(8,128)(2,1)}) custom-call(s32[8,8]{1,0:T(8,128)} %table.1, s32[8]{0:T(128)} %lens.1, bf16[8,3072]{1,0:T(8,128)(2,1)} %q_ref.1, bf16[64,16,512]{2,1,0:T(8,128)(2,1)} %pk_ref.1, bf16[64,16,512]{2,1,0:T(8,128)(2,1)} %pv_ref.1, ...), custom_call_target="tpu_custom_call" | custom-call | tf_op jit(solution)/shard_map/pallas_call | solution.py:397
  53.0 1.7 %shard_map.158 = (bf16[8,3072]{1,0:T(8,128)(2,1)}, bf16[1,128,512]{2,1,0:T(8,128)(2,1)}, bf16[1,128,512]{2,1,0:T(8,128)(2,1)}) custom-call(bf16[8,3072]{1,0:T(8,128)(2,1)} %get-tuple-element.6.refs_0_, bf16[1,128,512]{2,1,0:T(8,128)(2,1)} %get-tuple-element.7.refs_1_, bf16[1,128,512]{2,1,0:T(8,128)(2,1)} %get-tuple-element.8.refs_2_), custom_call_target="tpu_custom_call" | custom-call | tf_op jit(solution)/shard_map/pallas_call | solution.py:440
